TPU v7x, 32 devices: a whole 2x2x4 slice. The times are simulated.
32 devices in a mesh: groups: 2 (over y), edge: 4 (over z), expert: 2 (over x), sys: 2 (over core).
Axes of the slice: x: 2, y: 2, z: 4, core: 2. Of those that a mesh axis runs over, the one named last changes fastest.
Arguments:
- edge_inputs: bfloat16 [8, 1792, 1280], P(('groups', 'expert', 'sys'), 'edge'), parts along dimension 0, may hold values from -6 to 6
- out_grad: bfloat16 [8, 1792, 1152], P(('groups', 'expert', 'sys'), 'edge'), parts along dimension 0, may hold values from -6 to 6
- expert_weights: bfloat16 [32, 1280, 1152], P('expert', 'edge'), may hold values from -0.15625 to 0.15625
- coef_table: float32 [16, 32], replicated, may hold values from 0.05 to 0.5
- system_kind: int32 [8], P('groups'), parts along dimension 0, may hold values from 0 to 15
- edge_counts: int32 [8], P('groups'), parts along dimension 0, may hold values from 896 to 1792, as said below
Outputs:
- input_grad: bfloat16 [8, 1792, 1280], P(('groups', 'expert', 'sys'), 'edge'), parts along dimension 0
- weight_grad: bfloat16 [64, 1280, 1152], P(('groups', 'expert'), 'edge'), parts along dimension 0
There are 2 independent parts, one for each index of `groups`. A program takes and returns all parts, laid end to end along the dimension named above; an argument that names none is the same for every part. Nothing has to cross between parts.
Inputs may be any that keep to these rules, and one draw needn't show every extreme that they name: `edge_counts`: the live edges of a system are its first ones. One system has all 1792 slots live and another exactly half of them.
All inputs are finite; a program needn't handle non-finite values.
Results may differ from a plain program's by a relative error of at most 0.018.
Values may be sent and summed in bfloat16 or wider, within the bound.
A program may use at most 128 MiB of HBM per device.

v0:
```python
import math

import jax
import jax.numpy as jnp
from jax import lax
from jax.sharding import PartitionSpec as P


def body(edge_inputs, out_grad, expert_weights, coef_table, system_kind, edge_counts):
    highest = lax.Precision.HIGHEST
    edge_size = lax.axis_size("edge")
    expert_size = lax.axis_size("expert")
    sys_size = lax.axis_size("sys")
    edge_at = lax.axis_index("edge")
    expert_at = lax.axis_index("expert")
    sys_at = lax.axis_index("sys")
    systems = system_kind.shape[0]
    kinds = coef_table.shape[0]
    exp_local = expert_weights.shape[0]
    row_count = expert_weights.shape[1]
    width_out = expert_weights.shape[2]
    edge_rows = out_grad.shape[1]
    onehot = (system_kind[:, None] == jnp.arange(kinds, dtype=jnp.int32)[None, :]).astype(
        jnp.float32
    )
    coeffs = jnp.dot(onehot, coef_table, precision=highest)
    own_system = expert_at * sys_size + sys_at
    picked = jnp.arange(systems, dtype=jnp.int32) == own_system
    own_count = jnp.sum(jnp.where(picked, edge_counts, 0))
    positions = edge_at * edge_rows + jnp.arange(edge_rows, dtype=jnp.int32)
    masked_grad = jnp.where(
        (positions < own_count)[:, None], out_grad[0], jnp.zeros((), jnp.bfloat16)
    )
    features = edge_inputs[0]
    by_block = coeffs.reshape(expert_size, sys_size, -1)
    same_sys = lax.dynamic_slice_in_dim(by_block, sys_at, 1, 1)[:, 0, :]
    own_coeffs = lax.dynamic_slice_in_dim(same_sys, expert_at * exp_local, exp_local, 1)
    partials = jnp.sum(
        own_coeffs[:, :, None, None] * expert_weights.astype(jnp.float32)[None], axis=1
    ).astype(jnp.bfloat16)
    merged_rows = jnp.sum(
        lax.all_to_all(partials, "expert", split_axis=0, concat_axis=0, tiled=True).astype(
            jnp.float32
        ),
        axis=0,
    ).astype(jnp.bfloat16)
    product = lax.dot_general(
        masked_grad,
        lax.all_gather(merged_rows, "edge", axis=0, tiled=True),
        (((1,), (1,)), ((), ())),
        preferred_element_type=jnp.float32,
    )
    input_grad = product.astype(jnp.bfloat16)
    system_rows = lax.psum_scatter(
        lax.dot_general(
            features, masked_grad, (((0,), (0,)), ((), ())), preferred_element_type=jnp.float32
        ).astype(jnp.bfloat16),
        "edge",
        scatter_dimension=0,
        tiled=True,
    )
    local_coeffs = lax.dynamic_slice_in_dim(coeffs, expert_at * exp_local, exp_local, 1).T
    block_rows = lax.all_gather(system_rows[None], ("expert", "sys"), axis=0, tiled=True)
    span_rows = block_rows.shape[0]
    flat_rows = block_rows.reshape(span_rows, -1).astype(jnp.float32)
    folded = jnp.dot(local_coeffs, flat_rows, precision=highest)
    scale_factor = 1.0 / math.sqrt(edge_rows * edge_size)
    weight_grad = (
        (folded * scale_factor).reshape(exp_local, row_count, width_out).astype(jnp.bfloat16)
    )
    return (input_grad[None], weight_grad)


def solution(mesh):
    return jax.shard_map(
        body,
        mesh=mesh,
        in_specs=(
            P(("groups", "expert", "sys"), "edge", None),
            P(("groups", "expert", "sys"), "edge", None),
            P("expert", "edge", None),
            P(),
            P("groups"),
            P("groups"),
        ),
        out_specs=(
            P(("groups", "expert", "sys"), "edge", None),
            P(("groups", "expert"), "edge", None),
        ),
        check_vma=False,
    )
```

profile of v0, /device:TPU:0, one launch (start us, length us, event | category | flops | bytes accessed | tf_op | source)
XLA Modules:
  0.0 198.6 jit_solution(15670721173112743282)
XLA Ops:
  7.2 0.0 copy-start
  7.2 0.0 reduce-scatter.4.cloned.1.call-start
  7.2 1.4 fusion.13
  8.6 0.7 add_compare_fusion
  9.3 0.0 copy-done
  9.3 4.7 %fusion.1 = bf16[1280,1152]{0,1:T(8,128)(2,1)} fusion(bf16[1,448,1280]{2,1,0:T(8,128)(2,1)S(1)} %copy-done, bf16[1,448,1152]{2,1,0:T(8,128)(2,1)} %param.7, pred[448]{0:T(512)(128)(4,1)S(1)} %add_compare_fusion), kind=kOutput, calls=%fused_computation.4 | convolution fusion | flops 1323196416 | bytes 5128640 | tf_op jit(solution)/shard_map/dot_general | solution.py:55
  13.9 5.4 %copy.11 = bf16[1280,1152]{1,0:T(8,128)(2,1)} copy(bf16[1280,1152]{0,1:T(8,128)(2,1)} %fusion.1) | data formatting | bytes 5898240
  19.4 0.0 reduce-scatter.4.cloned.1.call-update
  19.4 0.0 all-gather.4.cloned.1.call-start
  19.5 0.0 copy-start.3
  19.5 0.0 copy-start.4
  19.5 13.6 %convert_element_type.25 = f32[16,320,1152]{2,1,0:T(8,128)} convert(bf16[16,320,1152]{2,1,0:T(8,128)(2,1)} %param.8) | non-fusion elementwise | flops 5898240 | bytes 35389440 | tf_op jit(solution)/shard_map/convert_element_type | solution.py:39
  33.1 0.0 copy-done.3
  33.1 0.0 copy-done.4
  33.1 0.2 fusion.11
  33.3 0.1 constant_dynamic-slice_fusion
  33.4 13.5 %multiply_reduce_fusion = bf16[2,320,1152]{2,1,0:T(8,128)(2,1)S(1)} fusion(f32[16,320,1152]{2,1,0:T(8,128)} %convert_element_type.25, f32[2,16]{1,0:T(2,128)S(1)} %bitcast.24), kind=kLoop, calls=%fused_computation.2 | loop fusion | flops 22855680 | bytes 25067648 | tf_op jit(solution)/shard_map/reduce_sum | solution.py:38
  46.9 0.0 copy-start.2
  46.9 22.3 %all_to_all.5 = bf16[2,320,1152]{2,1,0:T(8,128)(2,1)S(1)} all-to-all(bf16[2,320,1152]{2,1,0:T(8,128)(2,1)S(1)} %multiply_reduce_fusion), channel_id=1, replica_groups=mesh['groups'=2,'edge'=4,'expert'=2,'sys'=2] {'expert'}, dimensions={0} | all-to-all | bytes 2949120 | tf_op jit(solution)/shard_map/all_to_all | solution.py:42
  69.2 1.3 reduce_sum.32
  70.5 0.0 all-gather.4.cloned.1.call-update
  70.5 0.0 all-gather.6.cloned.1.call-start
  70.6 8.9 %reduce-scatter.4.cloned.1.call-done = bf16[320,1152]{1,0:T(8,128)(2,1)} async-done(((bf16[1280,1152]{1,0:T(8,128)(2,1)}), bf16[320,1152]{1,0:T(8,128)(2,1)}) %reduce-scatter.4.cloned.1.call-update) | async-done | bytes 737296 | tf_op jit(solution)/shard_map/reduce_scatter | solution.py:54
  79.5 0.0 all-gather.6.cloned.1.call-update
  79.5 62.4 %all-gather.4.cloned.1.call-done = bf16[1280,1152]{1,0:T(8,128)(2,1)} async-done(((bf16[320,1152]{1,0:T(8,128)(2,1)}), bf16[1280,1152]{1,0:T(8,128)(2,1)}) %all-gather.4.cloned.1.call-update) | async-done | bytes 2949136 | tf_op jit(solution)/shard_map/all_gather | solution.py:49
  141.9 0.0 copy-done.2
  141.9 4.6 %fusion.2 = bf16[1,448,1280]{2,1,0:T(8,128)(2,1)} fusion(bf16[1280,1152]{1,0:T(8,128)(2,1)} %all-gather.4.cloned.1.call-done, bf16[1,448,1152]{2,1,0:T(8,128)(2,1)S(1)} %copy-done.2, pred[448]{0:T(512)(128)(4,1)S(1)} %add_compare_fusion), kind=kOutput, calls=%fused_computation.6 | convolution fusion | flops 1322295296 | bytes 5128640 | tf_op jit(solution)/shard_map/dot_general | solution.py:47
  146.4 23.2 %all-gather.6.cloned.1.call-done = bf16[1280,1152]{1,0:T(8,128)(2,1)} async-done(((bf16[320,1152]{1,0:T(8,128)(2,1)}), bf16[1280,1152]{1,0:T(8,128)(2,1)}) %all-gather.6.cloned.1.call-update) | async-done | bytes 2949136 | tf_op jit(solution)/shard_map/all_gather | solution.py:63
  169.6 4.5 %reshape.31 = bf16[4,368640]{1,0:T(4,128)(2,1)} reshape(bf16[1280,1152]{1,0:T(8,128)(2,1)} %all-gather.6.cloned.1.call-done) | data formatting | bytes 5898240 | tf_op jit(solution)/shard_map/reshape | solution.py:65
  174.2 12.6 %fusion = bf16[16,368640]{1,0:T(8,128)(2,1)S(1)} fusion(bf16[4,368640]{1,0:T(4,128)(2,1)} %reshape.31, f32[4,32]{1,0:T(4,128)S(1)} %fusion.11, s32[]{:T(128)S(6)} %select_n.28), kind=kOutput, calls=%fused_computation.1 | convolution fusion | flops 294912000 | bytes 14746116 | tf_op jit(solution)/shard_map/dot_general | solution.py:66
  186.8 0.0 copy-start.1
  186.8 5.3 %copy.13 = bf16[2,8,320,1152]{3,2,1,0:T(8,128)(2,1)} copy(bf16[2,8,320,1152]{3,1,2,0:T(8,128)(2,1)S(1)} %bitcast.21) | data formatting | bytes 23592960
  192.0 0.0 copy-done.1
Async XLA Ops:
  7.2 2.1 %copy-start = (bf16[1,448,1280]{2,1,0:T(8,128)(2,1)S(1)}, bf16[1,448,1280]{2,1,0:T(8,128)(2,1)}, u32[]{:S(2)}) copy-start(bf16[1,448,1280]{2,1,0:T(8,128)(2,1)} %param.6) | copy-start | bytes 3440644
  7.2 72.3 %reduce-scatter.4.cloned.1.call-start = ((), (), s32[]{:S(2)}) async-start(), calls=%async_computation.4 | async-start | bytes 3686400 | tf_op jit(solution)/shard_map/reduce_scatter | solution.py:54
  19.4 122.5 %all-gather.4.cloned.1.call-start = ((), (), s32[]{:S(2)}) async-start(), calls=%async_computation.2 | async-start | bytes 3686400 | tf_op jit(solution)/shard_map/all_gather | solution.py:49
  19.5 13.7 %copy-start.3 = (f32[16,32]{1,0:T(8,128)S(1)}, f32[16,32]{1,0:T(8,128)}, u32[]{:S(2)}) copy-start(f32[16,32]{1,0:T(8,128)} %param.9) | copy-start | bytes 6148
  19.5 13.7 %copy-start.4 = (s32[4]{0:T(128)S(1)}, s32[4]{0:T(128)}, u32[]{:S(2)}) copy-start(s32[4]{0:T(128)} %param.10) | copy-start | bytes 52
  46.9 95.0 %copy-start.2 = (bf16[1,448,1152]{2,1,0:T(8,128)(2,1)S(1)}, bf16[1,448,1152]{2,1,0:T(8,128)(2,1)}, u32[]{:S(2)}) copy-start(bf16[1,448,1152]{2,1,0:T(8,128)(2,1)} %param.7) | copy-start | bytes 3096580
  70.5 99.1 %all-gather.6.cloned.1.call-start = ((), (), s32[]{:S(2)}) async-start(), calls=%async_computation.3 | async-start | bytes 3686400 | tf_op jit(solution)/shard_map/all_gather | solution.py:63
  186.8 5.3 %copy-start.1 = (bf16[1,448,1280]{2,1,0:T(8,128)(2,1)S(1)}, bf16[1,448,1280]{2,1,0:T(8,128)(2,1)}, u32[]{:S(2)}) copy-start(bf16[1,448,1280]{2,1,0:T(8,128)(2,1)} %param.6) | copy-start | bytes 3440644
Sparse Core Ops, SparseCore 0:
  19.5 59.9 reduce-scatter.3
  81.7 60.1 all-gather.3
  143.5 26.0 all-gather.5
where the time goes:
time: 199 us
  waiting for transfers between devices  94.5 us (47%)
  other arithmetic  30.4 us (15%)
  blocking collectives  22.3 us (11%)
  matrix products  22 us (11%)
  local copies, waits for them, and re-layouts  15.3 us (8%)
  between operations  13.8 us (7%)
    all_gather x1, waiting for transfers between devices, body(): lax.all_gather(merged_rows, 'edge', axis=0, tiled=True)  62.4 us
    all_gather x1, waiting for transfers between devices, body(): lax.all_gather(system_rows[None], ('expert', 'sys'), axis=0, tiled=True)  23.2 us
    all_to_all x1, blocking collectives, body(): lax.all_to_all(partials, 'expert', split_axis=0, concat_axis=0, tiled=True)  22.3 us
    convert_element_type x1, other arithmetic, body(): expert_weights.astype(jnp.float32)[None]  13.6 us
    reduce_sum x1, other arithmetic, body(): jnp.sum(own_coeffs[:, :, None, None] * expert_weights.astype(jnp.float32)...  13.5 us
    dot_general x1, matrix products, body(): folded = jnp.dot(local_coeffs, flat_rows, precision=highest)  12.6 us
    unnamed x12, local copies, waits for them, and re-layouts  10.7 us
    reduce_scatter x1, waiting for transfers between devices, body(): lax.psum_scatter(lax.dot_general(features, masked_grad, (((0,), (0,)), ((...  8.89 us
  transfers between devices with their start and end apart: 3, of which 3 were waited for; matrix products, arithmetic and copies ran while one was open for 17% of the time, Pallas kernels for 0%

commit v1 on v0

v1 whole, which is shorter than its diff:
```python
import functools
import math

import jax
import jax.numpy as jnp
from jax import lax
from jax.experimental import pallas as pl
from jax.experimental.pallas import tpu as pltpu
from jax.sharding import PartitionSpec as P

MESH = pl.DeviceIdType.MESH
F32 = jnp.float32
BF16 = jnp.bfloat16


def split_rows(rows, most):
    sizes = [size for size in range(16, min(rows, most) + 1, 16) if rows % size == 0]
    return max(sizes) if sizes else rows


def lane_tile(width):
    return 256 if width % 256 == 0 else 128 if width % 128 == 0 else width


def exchange(
    n_edge, n_expert, n_sys, piece,
    kind_ref, count_ref, table_ref, feat_any, grad_any, weight_any,
    input_grad_ref, blocks_any,
    feat, grad, weight, prod, from_left, from_right, merged, part_out, part_in, final,
    load_sem, weight_sem, part_send, part_recv,
    sum_send, sum_recv, all_send, all_recv,
    peer_send, peer_recv, core_send, core_recv, own_sem,
):
    z = lax.axis_index("edge")
    x = lax.axis_index("expert")
    core = lax.axis_index("sys")
    own_system = x * n_sys + core
    rows = weight.shape[1]
    pieces = rows // piece
    n_exp = weight.shape[0]
    width = weight.shape[2]
    edge_rows, depth = feat.shape
    lanes = 384 if width % 384 == 0 else lane_tile(width)

    feat_copy = pltpu.make_async_copy(feat_any.at[0], feat, load_sem.at[0])
    grad_copy = pltpu.make_async_copy(grad_any.at[0], grad, load_sem.at[1])
    grad_copy.start()
    feat_copy.start()

    def weight_copy(c):
        span = pl.ds(c * piece, piece)
        return pltpu.make_async_copy(
            weight_any.at[:, span, :], weight.at[:, span, :], weight_sem.at[c]
        )

    for c in range(pieces):
        weight_copy(c).start()

    barrier = pltpu.get_barrier_semaphore()

    @pl.when(z > 0)
    def _():
        pl.semaphore_signal(barrier, inc=1, device_id={"edge": z - 1}, device_id_type=MESH)

    @pl.when(z < n_edge - 1)
    def _():
        pl.semaphore_signal(barrier, inc=1, device_id={"edge": z + 1}, device_id_type=MESH)

    for t in range(n_expert):
        @pl.when(x != t)
        def _():
            pl.semaphore_signal(barrier, inc=1, device_id={"expert": t}, device_id_type=MESH)
    for t in range(n_sys):
        @pl.when(core != t)
        def _():
            pl.semaphore_signal(barrier, inc=1, device_id={"sys": t}, device_id_type=MESH)
    neighbours = jnp.where(z > 0, 1, 0) + jnp.where(z < n_edge - 1, 1, 0)
    pl.semaphore_wait(barrier, neighbours + (n_expert - 1) + (n_sys - 1))

    grad_copy.wait()
    live = count_ref[own_system] - z * edge_rows
    mask_rows = split_rows(edge_rows, 64)

    def mask_step(i, carry):
        at = pl.multiple_of(i * mask_rows, mask_rows)
        span = pl.ds(at, mask_rows)
        place = at + lax.broadcasted_iota(jnp.int32, (mask_rows, width), 0)
        values = grad[span, :].astype(F32)
        grad[span, :] = jnp.where(place < live, values, 0.0).astype(BF16)
        return carry

    lax.fori_loop(0, edge_rows // mask_rows, mask_step, 0)
    feat_copy.wait()

    tile = lane_tile(depth)

    def product_step(i, carry):
        span = pl.ds(pl.multiple_of(i * tile, tile), tile)
        prod[span, :] = lax.dot_general(
            feat[:, span], grad[...], (((0,), (0,)), ((), ())), preferred_element_type=F32
        ).astype(BF16)
        return carry

    lax.fori_loop(0, depth // tile, product_step, 0)

    def block(j, c):
        start = j * rows + c * piece
        return pl.ds(start if isinstance(start, int) else pl.multiple_of(start, 16), piece)

    def sum_copy(way, j, c):
        landing = from_left if way == 0 else from_right
        target = z + 1 if way == 0 else z - 1
        sem = (way * n_edge + j) * pieces + c
        return pltpu.make_async_remote_copy(
            src_ref=prod.at[block(j, c)],
            dst_ref=landing.at[block(j, c)],
            send_sem=sum_send.at[sem],
            recv_sem=sum_recv.at[sem],
            device_id={"edge": target},
            device_id_type=MESH,
        )

    def sum_step(m, c):
        high, low = n_edge - 1 - m, m

        @pl.when(z < high)
        def _():
            @pl.when(z > 0)
            def _():
                sum_copy(0, high, c).wait_recv()
                span = block(high, c)
                prod[span, :] = (
                    prod[span, :].astype(F32) + from_left[span, :].astype(F32)
                ).astype(BF16)

            sum_copy(0, high, c).start()

        @pl.when(z > low)
        def _():
            @pl.when(z < n_edge - 1)
            def _():
                sum_copy(1, low, c).wait_recv()
                span = block(low, c)
                prod[span, :] = (
                    prod[span, :].astype(F32) + from_right[span, :].astype(F32)
                ).astype(BF16)

            sum_copy(1, low, c).start()

    def peer_copy(t, source, c):
        span = pl.ds(c * piece, piece)
        return pltpu.make_async_remote_copy(
            src_ref=final.at[span],
            dst_ref=blocks_any.at[source * n_sys + core, span],
            send_sem=peer_send.at[t * pieces + c],
            recv_sem=peer_recv.at[source * pieces + c],
            device_id={"expert": t},
            device_id_type=MESH,
        )

    def core_copy(t, source, from_core, c, own):
        span = pl.ds(c * piece, piece)
        place = blocks_any.at[source * n_sys + from_core, span]
        return pltpu.make_async_remote_copy(
            src_ref=final.at[span] if own else place,
            dst_ref=place,
            send_sem=core_send.at[(t * n_expert + source) * pieces + c],
            recv_sem=core_recv.at[(from_core * n_expert + source) * pieces + c],
            device_id={"sys": t},
            device_id_type=MESH,
        )

    def own_copy(c):
        span = pl.ds(c * piece, piece)
        return pltpu.make_async_copy(
            final.at[span], blocks_any.at[own_system, span], own_sem.at[c]
        )

    def final_step(c):
        @pl.when(z > 0)
        def _():
            sum_copy(0, z, c).wait_recv()

        @pl.when(z < n_edge - 1)
        def _():
            sum_copy(1, z, c).wait_recv()

        span = block(z, c)
        out = pl.ds(c * piece, piece)

        @pl.when(z == 0)
        def _():
            final[out, :] = (
                prod[span, :].astype(F32) + from_right[span, :].astype(F32)
            ).astype(BF16)

        @pl.when(z == n_edge - 1)
        def _():
            final[out, :] = (
                prod[span, :].astype(F32) + from_left[span, :].astype(F32)
            ).astype(BF16)

        @pl.when(jnp.logical_and(z > 0, z < n_edge - 1))
        def _():
            final[out, :] = (
                prod[span, :].astype(F32)
                + from_left[span, :].astype(F32)
                + from_right[span, :].astype(F32)
            ).astype(BF16)

        for t in range(n_expert):
            @pl.when(x != t)
            def _():
                peer_copy(t, x, c).start()
        for t in range(n_sys):
            @pl.when(core != t)
            def _():
                core_copy(t, x, core, c, True).start()
        own_copy(c).start()

    def part_copy(t, source, c):
        span = pl.ds(c * piece, piece)
        return pltpu.make_async_remote_copy(
            src_ref=part_out.at[t, span],
            dst_ref=part_in.at[source, span],
            send_sem=part_send.at[t * pieces + c],
            recv_sem=part_recv.at[source * pieces + c],
            device_id={"expert": t},
            device_id_type=MESH,
        )

    kinds = [kind_ref[t * n_sys + core] for t in range(n_expert)]
    gains = [
        [table_ref[kinds[t], x * n_exp + e] for e in range(n_exp)] for t in range(n_expert)
    ]

    def part_step(c):
        weight_copy(c).wait()

        def row_step(i, carry):
            span = pl.ds(pl.multiple_of(c * piece + i * 16, 16), 16)
            for col in range(0, width, lanes):
                cols = slice(col, col + lanes)
                sums = [None] * n_expert
                for e in range(n_exp):
                    value = weight[e, span, cols].astype(F32)
                    for t in range(n_expert):
                        term = value * gains[t][e]
                        sums[t] = term if sums[t] is None else sums[t] + term
                for t in range(n_expert):
                    part_out[t, span, cols] = sums[t].astype(BF16)
            return carry

        lax.fori_loop(0, piece // 16, row_step, 0)
        for t in range(n_expert):
            @pl.when(x != t)
            def _():
                part_copy(t, x, c).start()

    def all_copy(way, j, c):
        target = z + 1 if way == 0 else z - 1
        sem = (way * n_edge + j) * pieces + c
        return pltpu.make_async_remote_copy(
            src_ref=merged.at[block(j, c)],
            dst_ref=merged.at[block(j, c)],
            send_sem=all_send.at[sem],
            recv_sem=all_recv.at[sem],
            device_id={"edge": target},
            device_id_type=MESH,
        )

    def all_first(c):
        span = pl.ds(c * piece, piece)
        for b in range(n_expert):
            @pl.when(x != b)
            def _():
                part_copy(b, b, c).wait_recv()
        total = part_out[x, span, :].astype(F32)
        for step in range(1, n_expert):
            total += part_in[lax.rem(x + step, n_expert), span, :].astype(F32)
        merged[block(z, c), :] = total.astype(BF16)

        @pl.when(z < n_edge - 1)
        def _():
            all_copy(0, z, c).start()

        @pl.when(z > 0)
        def _():
            all_copy(1, z, c).start()

    def all_step(m, c):
        @pl.when(z - m >= 0)
        def _():
            all_copy(0, z - m, c).wait_recv()

            @pl.when(z < n_edge - 1)
            def _():
                all_copy(0, z - m, c).start()

        @pl.when(z + m < n_edge)
        def _():
            all_copy(1, z + m, c).wait_recv()

            @pl.when(z > 0)
            def _():
                all_copy(1, z + m, c).start()

    for m in range(n_edge):
        if m == 0:
            @pl.when(jnp.logical_or(z == 0, z == n_edge - 1))
            def _():
                for c in range(pieces):
                    @pl.when(z == 0)
                    def _():
                        sum_copy(0, n_edge - 1, c).start()

                    @pl.when(z == n_edge - 1)
                    def _():
                        sum_copy(1, 0, c).start()

            for c in range(pieces):
                part_step(c)
            for c in range(pieces):
                @pl.when(jnp.logical_and(z > 0, z < n_edge - 1))
                def _():
                    sum_step(0, c)
        elif m < n_edge - 1:
            for c in range(pieces):
                sum_step(m, c)
        for c in range(pieces):
            if m == 0:
                all_first(c)
            else:
                all_step(m, c)
        if m == max(n_edge - 2, 0):
            for c in range(pieces):
                final_step(c)

    for c in range(pieces):
        for b in range(n_expert):
            @pl.when(x != b)
            def _():
                peer_copy(b, b, c).wait_recv()
                for t in range(n_sys):
                    @pl.when(core != t)
                    def _():
                        core_copy(t, b, core, c, False).start()

    def input_step(i, carry):
        span = pl.ds(pl.multiple_of(i * tile, tile), tile)
        input_grad_ref[0, :, span] = lax.dot_general(
            grad[...], merged[span, :], (((1,), (1,)), ((), ())), preferred_element_type=F32
        ).astype(BF16)
        return carry

    lax.fori_loop(0, depth // tile, input_step, 0)

    for c in range(pieces):
        own_copy(c).wait()
        for t in range(n_expert):
            @pl.when(x != t)
            def _():
                peer_copy(t, x, c).wait_send()
                part_copy(t, x, c).wait_send()
        for t in range(n_sys):
            @pl.when(core != t)
            def _():
                for b in range(n_expert):
                    core_copy(t, b, t, c, False).wait_recv()
                    core_copy(t, b, core, c, False).wait_send()
        for j in range(n_edge):
            @pl.when(z < j)
            def _():
                sum_copy(0, j, c).wait_send()

            @pl.when(z > j)
            def _():
                sum_copy(1, j, c).wait_send()

            @pl.when(jnp.logical_and(j <= z, z < n_edge - 1))
            def _():
                all_copy(0, j, c).wait_send()

            @pl.when(jnp.logical_and(j >= z, z > 0))
            def _():
                all_copy(1, j, c).wait_send()


def expand(n_sys, scale, kind_ref, table_ref, block_ref, out_ref, gains):
    systems, rows, width = block_ref.shape
    n_exp = out_ref.shape[0]
    x = lax.axis_index("expert")
    depth = systems * rows

    @pl.when(pl.program_id(0) == 0)
    def _():
        lane = lax.broadcasted_iota(jnp.int32, (rows, depth), 1)
        row = lax.broadcasted_iota(jnp.int32, (rows, depth), 0)
        for e in range(n_exp):
            values = jnp.zeros((rows, depth), F32)
            for s in range(systems):
                gain = table_ref[kind_ref[s], x * n_exp + e] * scale
                values = jnp.where(lane == row + s * rows, gain, values)
            gains[pl.ds(e * rows, rows), :] = values.astype(BF16)

    stacked = block_ref[...].reshape(depth, width)
    group = max(1, min(n_exp, 256 // rows))
    while n_exp % group:
        group -= 1

    def step(i, carry):
        at = pl.multiple_of(i * group * rows, 16)
        result = jnp.dot(
            gains[pl.ds(at, group * rows), :], stacked, preferred_element_type=F32
        )
        out_ref[pl.ds(i * group, group)] = result.astype(BF16).reshape(group, rows, width)
        return carry

    lax.fori_loop(0, n_exp // group, step, 0)


def body(edge_inputs, out_grad, expert_weights, coef_table, system_kind, edge_counts):
    n_edge = lax.axis_size("edge")
    n_expert = lax.axis_size("expert")
    n_sys = lax.axis_size("sys")
    systems = system_kind.shape[0]
    n_exp, rows, width = expert_weights.shape
    edge_rows, depth = edge_inputs.shape[1:]
    piece = split_rows(rows, 80)
    pieces = rows // piece
    dma = lambda count: pltpu.SemaphoreType.DMA((count,))
    smem = pl.BlockSpec(memory_space=pltpu.SMEM)
    anywhere = pl.BlockSpec(memory_space=pl.ANY)
    vmem = pl.BlockSpec(memory_space=pltpu.VMEM)
    input_grad, blocks = pl.pallas_call(
        functools.partial(exchange, n_edge, n_expert, n_sys, piece),
        out_shape=(
            jax.ShapeDtypeStruct((1, edge_rows, depth), BF16),
            jax.ShapeDtypeStruct((systems, rows, width), BF16),
        ),
        in_specs=[smem, smem, smem, anywhere, anywhere, anywhere],
        out_specs=(vmem, anywhere),
        scratch_shapes=[
            pltpu.VMEM((edge_rows, depth), BF16),
            pltpu.VMEM((edge_rows, width), BF16),
            pltpu.VMEM((n_exp, rows, width), BF16),
            pltpu.VMEM((depth, width), BF16),
            pltpu.VMEM((depth, width), BF16),
            pltpu.VMEM((depth, width), BF16),
            pltpu.VMEM((depth, width), BF16),
            pltpu.VMEM((n_expert, rows, width), BF16),
            pltpu.VMEM((n_expert, rows, width), BF16),
            pltpu.VMEM((rows, width), BF16),
            dma(2),
            dma(pieces),
            dma(n_expert * pieces),
            dma(n_expert * pieces),
            dma(2 * n_edge * pieces),
            dma(2 * n_edge * pieces),
            dma(2 * n_edge * pieces),
            dma(2 * n_edge * pieces),
            dma(n_expert * pieces),
            dma(n_expert * pieces),
            dma(n_sys * n_expert * pieces),
            dma(n_sys * n_expert * pieces),
            dma(pieces),
        ],
        compiler_params=pltpu.CompilerParams(
            collective_id=0, has_side_effects=True, vmem_limit_bytes=50 * 2**20
        ),
        name="exchange",
    )(system_kind, edge_counts, coef_table, edge_inputs, out_grad, expert_weights)

    block_rows = split_rows(rows, max(16, 256 // systems))
    scale = 1.0 / math.sqrt(edge_rows * n_edge)
    weight_grad = pl.pallas_call(
        functools.partial(expand, n_sys, scale),
        grid=(rows // block_rows,),
        out_shape=jax.ShapeDtypeStruct((n_exp, rows, width), BF16),
        in_specs=[smem, smem, pl.BlockSpec((systems, block_rows, width), lambda i: (0, i, 0))],
        out_specs=pl.BlockSpec((n_exp, block_rows, width), lambda i: (0, i, 0)),
        scratch_shapes=[pltpu.VMEM((n_exp * block_rows, systems * block_rows), BF16)],
        compiler_params=pltpu.CompilerParams(vmem_limit_bytes=40 * 2**20),
        name="expand",
    )(system_kind, coef_table, blocks)
    return (input_grad, weight_grad)


def solution(mesh):
    return jax.shard_map(
        body,
        mesh=mesh,
        in_specs=(
            P(("groups", "expert", "sys"), "edge", None),
            P(("groups", "expert", "sys"), "edge", None),
            P("expert", "edge", None),
            P(),
            P("groups"),
            P("groups"),
        ),
        out_specs=(
            P(("groups", "expert", "sys"), "edge", None),
            P(("groups", "expert"), "edge", None),
        ),
        check_vma=False,
    )
```

time: 199 us -> 125 us (0.63)
  the two profiles are of different devices: /device:TPU:0 before, /device:TPU:8 now
where the time goes in v1:
time: 125 us
  Pallas kernels  117 us (94%)
  local copies, waits for them, and re-layouts  7.3 us (6%)
    pallas_call x1, Pallas kernels, body(): pl.pallas_call(functools.partial(exchange, n_edge, n_expert, n_sys, piece...  107 us
    pallas_call x1, Pallas kernels, body(): pl.pallas_call(functools.partial(expand, n_sys, scale), grid=(rows // blo...  9.89 us
    unnamed x13, local copies, waits for them, and re-layouts  7.3 us

profile of v1, /device:TPU:8, one launch (start us, length us, event | category | flops | bytes accessed | tf_op | source)
XLA Modules:
  0.0 125.0 jit_solution(7460218680918958157)
XLA Ops:
  0.6 0.0 copy-start.1
  0.6 1.2 copy-done.1
  1.9 0.0 copy-start.2
  1.9 1.2 copy-done.2
  3.1 0.0 copy-start.3
  3.1 0.7 copy-done.3
  3.8 0.0 copy-start.4
  3.8 0.7 copy-done.4
  4.5 0.0 copy-start.5
  4.5 0.7 copy-done.5
  5.1 107.2 %exchange.1 = (bf16[1,448,1280]{2,1,0:T(8,128)(2,1)S(1)}, bf16[4,320,1152]{2,1,0:T(8,128)(2,1)}) custom-call(s32[4]{0:T(128)S(1)} %copy-done.4, s32[4]{0:T(128)S(1)} %copy-done.5, f32[16,32]{1,0:T(8,128)S(1)} %copy-done.3, bf16[1,448,1280]{2,1,0:T(8,128)(2,1)S(1)} %copy-done.1, bf16[1,448,1152]{2,1,0:T(8,128)(2,1)S(1)} %copy-done.2, ...), custom_call_target="tpu_custom_call" | custom-call | tf_op jit(solution)/shard_map/exchange/pallas_call | solution.py:435
  112.3 0.0 copy-start
  112.3 1.8 %copy-done = bf16[4,320,1152]{2,1,0:T(8,128)(2,1)S(1)} copy-done((bf16[4,320,1152]{2,1,0:T(8,128)(2,1)S(1)}, bf16[4,320,1152]{2,1,0:T(8,128)(2,1)}, u32[]{:S(2)}) %copy-start) | copy-done | bytes 2949144
  114.2 9.9 %expand.1 = bf16[16,320,1152]{2,1,0:T(8,128)(2,1)} custom-call(s32[4]{0:T(128)S(1)} %copy-done.4, f32[16,32]{1,0:T(8,128)S(1)} %copy-done.3, bf16[4,320,1152]{2,1,0:T(8,128)(2,1)S(1)} %copy-done), custom_call_target="tpu_custom_call" | custom-call | tf_op jit(solution)/shard_map/expand/pallas_call | solution.py:476
  124.0 1.0 copy.9
Async XLA Ops:
  0.6 1.3 %copy-start.1 = (bf16[1,448,1280]{2,1,0:T(8,128)(2,1)S(1)}, bf16[1,448,1280]{2,1,0:T(8,128)(2,1)}, u32[]{:S(2)}) copy-start(bf16[1,448,1280]{2,1,0:T(8,128)(2,1)} %feat_any.1) | copy-start | bytes 3440644
  1.9 1.2 copy-start.2
  3.1 0.7 copy-start.3
  3.8 0.7 copy-start.4
  4.5 0.7 copy-start.5
  112.3 1.8 %copy-start = (bf16[4,320,1152]{2,1,0:T(8,128)(2,1)S(1)}, bf16[4,320,1152]{2,1,0:T(8,128)(2,1)}, u32[]{:S(2)}) copy-start(bf16[4,320,1152]{2,1,0:T(8,128)(2,1)} %get-tuple-element.5.block_ref) | copy-start | bytes 8847364

commit v2 on v1

--- a/solution.py
+++ b/solution.py
@@ -24,8 +24,9 @@
 
 def exchange(
     n_edge, n_expert, n_sys, piece,
-    kind_ref, count_ref, table_ref, feat_any, grad_any, weight_any,
+    kind_any, count_any, table_any, feat_any, grad_any, weight_any,
     input_grad_ref, blocks_any,
+    kind_ref, count_ref, table_ref,
     feat, grad, weight, prod, from_left, from_right, merged, part_out, part_in, final,
     load_sem, weight_sem, part_send, part_recv,
     sum_send, sum_recv, all_send, all_recv,
@@ -44,7 +45,15 @@
 
     feat_copy = pltpu.make_async_copy(feat_any.at[0], feat, load_sem.at[0])
     grad_copy = pltpu.make_async_copy(grad_any.at[0], grad, load_sem.at[1])
+    small_copies = [
+        pltpu.make_async_copy(source, target, load_sem.at[2 + i])
+        for i, (source, target) in enumerate(
+            ((count_any, count_ref), (kind_any, kind_ref), (table_any, table_ref))
+        )
+    ]
     grad_copy.start()
+    for copy in small_copies:
+        copy.start()
     feat_copy.start()
 
     def weight_copy(c):
@@ -77,6 +86,8 @@
     neighbours = jnp.where(z > 0, 1, 0) + jnp.where(z < n_edge - 1, 1, 0)
     pl.semaphore_wait(barrier, neighbours + (n_expert - 1) + (n_sys - 1))
 
+    for copy in small_copies:
+        copy.wait()
     grad_copy.wait()
     live = count_ref[own_system] - z * edge_rows
     mask_rows = split_rows(edge_rows, 64)
@@ -94,14 +105,19 @@
 
     tile = lane_tile(depth)
 
+    lower = z < n_edge // 2
+    tiles = depth // tile
+
     def product_step(i, carry):
-        span = pl.ds(pl.multiple_of(i * tile, tile), tile)
+        at = jnp.where(lower, tiles - 1 - i, i)
+        span = pl.ds(pl.multiple_of(at * tile, tile), tile)
         prod[span, :] = lax.dot_general(
             feat[:, span], grad[...], (((0,), (0,)), ((), ())), preferred_element_type=F32
         ).astype(BF16)
         return carry
 
-    lax.fori_loop(0, depth // tile, product_step, 0)
+    ahead = pl.cdiv(rows, tile)
+    lax.fori_loop(0, ahead, product_step, 0)
 
     def block(j, c):
         start = j * rows + c * piece
@@ -269,7 +285,7 @@
             device_id_type=MESH,
         )
 
-    def all_first(c):
+    def own_rows(c):
         span = pl.ds(c * piece, piece)
         for b in range(n_expert):
             @pl.when(x != b)
@@ -280,63 +296,32 @@
             total += part_in[lax.rem(x + step, n_expert), span, :].astype(F32)
         merged[block(z, c), :] = total.astype(BF16)
 
-        @pl.when(z < n_edge - 1)
-        def _():
-            all_copy(0, z, c).start()
-
-        @pl.when(z > 0)
-        def _():
-            all_copy(1, z, c).start()
-
-    def all_step(m, c):
-        @pl.when(z - m >= 0)
-        def _():
-            all_copy(0, z - m, c).wait_recv()
-
-            @pl.when(z < n_edge - 1)
-            def _():
-                all_copy(0, z - m, c).start()
-
-        @pl.when(z + m < n_edge)
-        def _():
-            all_copy(1, z + m, c).wait_recv()
-
-            @pl.when(z > 0)
-            def _():
-                all_copy(1, z + m, c).start()
-
-    for m in range(n_edge):
-        if m == 0:
-            @pl.when(jnp.logical_or(z == 0, z == n_edge - 1))
-            def _():
-                for c in range(pieces):
-                    @pl.when(z == 0)
-                    def _():
-                        sum_copy(0, n_edge - 1, c).start()
-
-                    @pl.when(z == n_edge - 1)
-                    def _():
-                        sum_copy(1, 0, c).start()
-
-            for c in range(pieces):
-                part_step(c)
-            for c in range(pieces):
-                @pl.when(jnp.logical_and(z > 0, z < n_edge - 1))
-                def _():
-                    sum_step(0, c)
-        elif m < n_edge - 1:
-            for c in range(pieces):
-                sum_step(m, c)
-        for c in range(pieces):
-            if m == 0:
-                all_first(c)
-            else:
-                all_step(m, c)
-        if m == max(n_edge - 2, 0):
-            for c in range(pieces):
-                final_step(c)
-
-    for c in range(pieces):
+    def own_send(way, c):
+        @pl.when(z < n_edge - 1 if way == 0 else z > 0)
+        def _():
+            all_copy(way, z, c).start()
+
+    def all_step(way, m, c):
+        j = z - m if way == 0 else z + m
+
+        @pl.when(j >= 0 if way == 0 else j < n_edge)
+        def _():
+            all_copy(way, j, c).wait_recv()
+
+            @pl.when(z < n_edge - 1 if way == 0 else z > 0)
+            def _():
+                all_copy(way, j, c).start()
+
+    def by_half(function, far, *args):
+        @pl.when(lower)
+        def _():
+            function(1 if far else 0, *args)
+
+        @pl.when(jnp.logical_not(lower))
+        def _():
+            function(0 if far else 1, *args)
+
+    def peer_step(c):
         for b in range(n_expert):
             @pl.when(x != b)
             def _():
@@ -345,6 +330,54 @@
                     @pl.when(core != t)
                     def _():
                         core_copy(t, b, core, c, False).start()
+
+    def end_sums(m):
+        for c in range(pieces):
+            @pl.when(z == 0)
+            def _():
+                sum_copy(0, n_edge - 1 - m, c).start()
+
+            @pl.when(z == n_edge - 1)
+            def _():
+                sum_copy(1, m, c).start()
+
+    inside = jnp.logical_and(z > 0, z < n_edge - 1)
+
+    def inside_sums(m, c):
+        @pl.when(inside)
+        def _():
+            sum_step(m, c)
+
+    end_sums(0)
+    lax.fori_loop(ahead, tiles, product_step, 0)
+    for m in range(1, n_edge - 1):
+        end_sums(m)
+
+    for c in range(pieces):
+        part_step(c)
+        if c > 0:
+            inside_sums(0, c - 1)
+    inside_sums(0, pieces - 1)
+    for c in range(pieces):
+        own_rows(c)
+        by_half(own_send, True, c)
+    for c in range(pieces):
+        if n_edge > 2:
+            inside_sums(1, c)
+        by_half(own_send, False, c)
+    for m in range(2, n_edge - 1):
+        for c in range(pieces):
+            inside_sums(m, c)
+    for c in range(pieces):
+        final_step(c)
+        by_half(all_step, True, 1, c)
+    for m in range(1, n_edge):
+        for c in range(pieces):
+            by_half(all_step, False, m, c)
+            if m + 1 < n_edge:
+                by_half(all_step, True, m + 1, c)
+            if m == 1:
+                peer_step(c)
 
     def input_step(i, carry):
         span = pl.ds(pl.multiple_of(i * tile, tile), tile)
@@ -408,15 +441,12 @@
     while n_exp % group:
         group -= 1
 
-    def step(i, carry):
-        at = pl.multiple_of(i * group * rows, 16)
+    for i in range(n_exp // group):
+        at = i * group * rows
         result = jnp.dot(
             gains[pl.ds(at, group * rows), :], stacked, preferred_element_type=F32
         )
         out_ref[pl.ds(i * group, group)] = result.astype(BF16).reshape(group, rows, width)
-        return carry
-
-    lax.fori_loop(0, n_exp // group, step, 0)
 
 
 def body(edge_inputs, out_grad, expert_weights, coef_table, system_kind, edge_counts):
@@ -438,9 +468,12 @@
             jax.ShapeDtypeStruct((1, edge_rows, depth), BF16),
             jax.ShapeDtypeStruct((systems, rows, width), BF16),
         ),
-        in_specs=[smem, smem, smem, anywhere, anywhere, anywhere],
+        in_specs=[anywhere] * 6,
         out_specs=(vmem, anywhere),
         scratch_shapes=[
+            pltpu.SMEM(system_kind.shape, jnp.int32),
+            pltpu.SMEM(edge_counts.shape, jnp.int32),
+            pltpu.SMEM(coef_table.shape, F32),
             pltpu.VMEM((edge_rows, depth), BF16),
             pltpu.VMEM((edge_rows, width), BF16),
             pltpu.VMEM((n_exp, rows, width), BF16),
@@ -451,7 +484,7 @@
             pltpu.VMEM((n_expert, rows, width), BF16),
             pltpu.VMEM((n_expert, rows, width), BF16),
             pltpu.VMEM((rows, width), BF16),
-            dma(2),
+            dma(5),
             dma(pieces),
             dma(n_expert * pieces),
             dma(n_expert * pieces),
@@ -466,7 +499,7 @@
             dma(pieces),
         ],
         compiler_params=pltpu.CompilerParams(
-            collective_id=0, has_side_effects=True, vmem_limit_bytes=50 * 2**20
+            collective_id=0, has_side_effects=True, vmem_limit_bytes=60 * 2**20
         ),
         name="exchange",
     )(system_kind, edge_counts, coef_table, edge_inputs, out_grad, expert_weights)
@@ -480,7 +513,7 @@
         in_specs=[smem, smem, pl.BlockSpec((systems, block_rows, width), lambda i: (0, i, 0))],
         out_specs=pl.BlockSpec((n_exp, block_rows, width), lambda i: (0, i, 0)),
         scratch_shapes=[pltpu.VMEM((n_exp * block_rows, systems * block_rows), BF16)],
-        compiler_params=pltpu.CompilerParams(vmem_limit_bytes=40 * 2**20),
+        compiler_params=pltpu.CompilerParams(vmem_limit_bytes=60 * 2**20),
         name="expand",
     )(system_kind, coef_table, blocks)
     return (input_grad, weight_grad)

time: 125 us -> 124 us (level)
  the two profiles are of different devices: /device:TPU:8 before, /device:TPU:0 now
where the time goes in v2:
time: 124 us
  Pallas kernels  122 us (98%)
    pallas_call x1, Pallas kernels, body(): pl.pallas_call(functools.partial(exchange, n_edge, n_expert, n_sys, piece...  114 us
    pallas_call x1, Pallas kernels, body(): pl.pallas_call(functools.partial(expand, n_sys, scale), grid=(rows // blo...  8.45 us

profile of v2, /device:TPU:0, one launch (start us, length us, event | category | flops | bytes accessed | tf_op | source)
XLA Modules:
  0.0 124.0 jit_solution(13185297022989011706)
XLA Ops:
  0.6 113.9 %exchange.1 = (bf16[1,448,1280]{2,1,0:T(8,128)(2,1)}, bf16[4,320,1152]{2,1,0:T(8,128)(2,1)}) custom-call(s32[4]{0:T(128)} %kind_ref.1, s32[4]{0:T(128)} %count_any.1, f32[16,32]{1,0:T(8,128)} %table_ref.1, bf16[1,448,1280]{2,1,0:T(8,128)(2,1)} %feat_any.1, bf16[1,448,1152]{2,1,0:T(8,128)(2,1)} %grad_any.1, bf16[16,320,1152]{2,1,0:T(8,128)(2,1)} %weight_any.1), custom_call_target="tpu_custom_call" | custom-call | tf_op jit(solution)/shard_map/exchange/pallas_call | solution.py:465
  114.6 0.0 copy-start
  114.6 8.4 %expand.1 = bf16[16,320,1152]{2,1,0:T(8,128)(2,1)} custom-call(s32[4]{0:T(128)} %kind_ref.1, f32[16,32]{1,0:T(8,128)} %table_ref.1, bf16[4,320,1152]{2,1,0:T(8,128)(2,1)} %get-tuple-element.5.block_ref), custom_call_target="tpu_custom_call" | custom-call | tf_op jit(solution)/shard_map/expand/pallas_call | solution.py:509
  123.0 0.0 copy-done
  123.0 1.0 copy.9
Async XLA Ops:
  114.6 8.5 %copy-start = (bf16[1,448,1280]{2,1,0:T(8,128)(2,1)S(1)}, bf16[1,448,1280]{2,1,0:T(8,128)(2,1)}, u32[]{:S(2)}) copy-start(bf16[1,448,1280]{2,1,0:T(8,128)(2,1)} %get-tuple-element.8) | copy-start | bytes 3440644

commit v3 on v2

--- a/solution.py
+++ b/solution.py
@@ -456,7 +456,7 @@
     systems = system_kind.shape[0]
     n_exp, rows, width = expert_weights.shape
     edge_rows, depth = edge_inputs.shape[1:]
-    piece = split_rows(rows, 80)
+    piece = split_rows(rows, 160)
     pieces = rows // piece
     dma = lambda count: pltpu.SemaphoreType.DMA((count,))
     smem = pl.BlockSpec(memory_space=pltpu.SMEM)

time: 124 us -> 121 us (0.976)
  Pallas kernels: 122 us -> 119 us
    pallas_call x1, Pallas kernels: 114 us -> 111 us  [body(): pl.pallas_call(functools.partial(exchange, n_edge, n_expert, n_sys, piece...]
where the time goes in v3:
time: 121 us
  Pallas kernels  119 us (98%)
    pallas_call x1, Pallas kernels, body(): pl.pallas_call(functools.partial(exchange, n_edge, n_expert, n_sys, piece...  111 us
    pallas_call x1, Pallas kernels, body(): pl.pallas_call(functools.partial(expand, n_sys, scale), grid=(rows // blo...  8.45 us

profile of v3, /device:TPU:0, one launch (start us, length us, event | category | flops | bytes accessed | tf_op | source)
XLA Modules:
  0.0 120.7 jit_solution(6976531395844905380)
XLA Ops:
  0.6 110.6 %exchange.1 = (bf16[1,448,1280]{2,1,0:T(8,128)(2,1)}, bf16[4,320,1152]{2,1,0:T(8,128)(2,1)}) custom-call(s32[4]{0:T(128)} %kind_ref.1, s32[4]{0:T(128)} %count_any.1, f32[16,32]{1,0:T(8,128)} %table_ref.1, bf16[1,448,1280]{2,1,0:T(8,128)(2,1)} %feat_any.1, bf16[1,448,1152]{2,1,0:T(8,128)(2,1)} %grad_any.1, bf16[16,320,1152]{2,1,0:T(8,128)(2,1)} %weight_any.1), custom_call_target="tpu_custom_call" | custom-call | tf_op jit(solution)/shard_map/exchange/pallas_call | solution.py:465
  111.2 0.0 copy-start
  111.2 8.4 %expand.1 = bf16[16,320,1152]{2,1,0:T(8,128)(2,1)} custom-call(s32[4]{0:T(128)} %kind_ref.1, f32[16,32]{1,0:T(8,128)} %table_ref.1, bf16[4,320,1152]{2,1,0:T(8,128)(2,1)} %get-tuple-element.5.block_ref), custom_call_target="tpu_custom_call" | custom-call | tf_op jit(solution)/shard_map/expand/pallas_call | solution.py:509
  119.7 0.0 copy-done
  119.7 1.0 copy.9
Async XLA Ops:
  111.2 8.5 %copy-start = (bf16[1,448,1280]{2,1,0:T(8,128)(2,1)S(1)}, bf16[1,448,1280]{2,1,0:T(8,128)(2,1)}, u32[]{:S(2)}) copy-start(bf16[1,448,1280]{2,1,0:T(8,128)(2,1)} %get-tuple-element.8) | copy-start | bytes 3440644
